TPU v7x, 256 devices: a whole 4x4x8 slice. The times are simulated.
256 devices in a mesh: seq: 8 (over z), head: 32 (over x, y, core).
Axes of the slice: x: 4, y: 4, z: 8, core: 2. Of those that a mesh axis runs over, the one named last changes fastest.
Arguments:
- projected: bfloat16 [2, 16384, 16384], P(None, ('seq', 'head')), may hold values from -6 to 6
- state_maps: bfloat16 [2, 16384, 4096], P(None, ('seq', 'head')), may hold values from -3 to 3
- step_raw: bfloat16 [2, 16384, 256], P(None, ('seq', 'head')), may hold values from -3 to 14
- step_bias: float32 [256], P('head'), may hold values from -9 to -2
- decay_rate: float32 [256], P('head'), may hold values from 0.1 to 2
- skip_gain: float32 [256], P('head'), may hold values from 0.5 to 1.5
- conv_weight: bfloat16 [4, 16384], P(None, 'head'), may hold values from -3 to 3
- conv_bias: float32 [16384], P('head'), may hold values from -1.5 to 1.5
- map_weight: bfloat16 [4, 4096], replicated, may hold values from -3 to 3
- map_bias: float32 [4096], replicated, may hold values from -1.5 to 1.5
Outputs:
- mixed_out: bfloat16 [2, 16384, 16384], P(None, ('seq', 'head'))
All inputs are finite; a program needn't handle non-finite values.
Results may differ from a plain program's by a relative error of at most 0.0057.
Values may be sent and summed in bfloat16 or wider, within the bound.
A program may use at most 128 MiB of HBM per device.

v0:
```python
import jax
import jax.numpy as jnp
from jax import lax
from jax.sharding import PartitionSpec as P

HEAD_DIM = 64
STATE = 256
GROUPS = 8
SPAN = 256
CONV = 4


def from_behind(array, axis, by):
    count = lax.axis_size(axis)
    pairs = [(i, i + by) for i in range(count) if 0 <= i + by < count]
    return lax.ppermute(array, axis, pairs)


def causal_conv(rim_rows, inner_rows, weight, bias):
    length = inner_rows.shape[1]
    window = jnp.concatenate([rim_rows, inner_rows], axis=1)
    total = bias
    for tap_index in range(CONV):
        part = lax.slice_in_dim(window, tap_index, tap_index + length, axis=1)
        total = total + weight[tap_index].astype(jnp.float32) * part.astype(jnp.float32)
    return jax.nn.silu(total).astype(jnp.bfloat16)


def local(
    projected,
    state_maps,
    step_raw,
    step_bias,
    decay_rate,
    skip_gain,
    conv_weight,
    conv_bias,
    map_weight,
    map_bias,
):
    head_count = lax.axis_size("head")
    heads_here = step_bias.shape[0]
    seq_count = projected.shape[0]
    row_count = projected.shape[1]
    width = heads_here * HEAD_DIM
    repeats = head_count // GROUPS
    group_index = lax.axis_index("head") // repeats
    grouped = state_maps.reshape(seq_count, row_count, 2, GROUPS, STATE).transpose(0, 1, 3, 2, 4)
    spread = jnp.broadcast_to(
        grouped[:, :, :, None], (seq_count, row_count, GROUPS, repeats, 2, STATE)
    )
    sent_maps = spread.reshape(seq_count, row_count, head_count * 2 * STATE)
    local_x, local_step, local_maps = (
        lax.all_to_all(projected, "head", split_axis=2, concat_axis=1, tiled=True),
        lax.all_to_all(step_raw, "head", split_axis=2, concat_axis=1, tiled=True),
        lax.all_to_all(sent_maps, "head", split_axis=2, concat_axis=1, tiled=True),
    )
    length = local_x.shape[1]
    map_taps = lax.dynamic_slice_in_dim(
        map_weight.reshape(CONV, 2, GROUPS, STATE), group_index, 1, 2
    ).reshape(CONV, 2 * STATE)
    map_shift = lax.dynamic_slice_in_dim(
        map_bias.reshape(2, GROUPS, STATE), group_index, 1, 1
    ).reshape(2 * STATE)
    rim_x, rim_maps = from_behind(
        (local_x[:, length - CONV + 1 :], local_maps[:, length - CONV + 1 :]), "seq", 1
    )
    inner_x = causal_conv(rim_x, local_x, conv_weight, conv_bias)
    inner_maps = causal_conv(rim_maps, local_maps, map_taps, map_shift)
    delta = jax.nn.softplus(local_step.astype(jnp.float32) + step_bias)
    log_decay = -delta * decay_rate
    span_count = length // SPAN
    x_spans = inner_x.reshape(seq_count, span_count, SPAN, heads_here, HEAD_DIM)
    b_spans = inner_maps[:, :, :STATE].reshape(seq_count, span_count, SPAN, STATE)
    c_spans = inner_maps[:, :, STATE:].reshape(seq_count, span_count, SPAN, STATE)
    delta_spans = delta.reshape(seq_count, span_count, SPAN, heads_here)
    cumulative = jnp.cumsum(log_decay.reshape(seq_count, span_count, SPAN, heads_here), axis=2)
    lower = lax.broadcasted_iota(jnp.int32, (SPAN, SPAN), 0) >= lax.broadcasted_iota(
        jnp.int32, (SPAN, SPAN), 1
    )

    def span_work(index):
        x_here = lax.dynamic_index_in_dim(x_spans, index, 1, keepdims=False)
        b_here = lax.dynamic_index_in_dim(b_spans, index, 1, keepdims=False)
        c_here = lax.dynamic_index_in_dim(c_spans, index, 1, keepdims=False)
        delta_here = lax.dynamic_index_in_dim(delta_spans, index, 1, keepdims=False)
        cum_here = lax.dynamic_index_in_dim(cumulative, index, 1, keepdims=False)
        scores = jnp.einsum("stn,skn->stk", c_here, b_here, preferred_element_type=jnp.float32)
        cum_heads = cum_here.transpose(0, 2, 1)
        differ = cum_heads[:, :, :, None] - cum_heads[:, :, None, :]
        decay = jnp.where(lower, jnp.exp(jnp.minimum(differ, 0.0)), 0.0)
        weights = (scores[:, None] * decay * delta_here.transpose(0, 2, 1)[:, :, None, :]).astype(
            jnp.bfloat16
        )
        intra = jnp.einsum("shtk,skhp->sthp", weights, x_here, preferred_element_type=jnp.float32)
        scale = jnp.exp(cum_here[:, -1:] - cum_here) * delta_here
        carried = (x_here * scale[..., None]).astype(jnp.bfloat16)
        produced = jnp.einsum("skhp,skn->shpn", carried, b_here, preferred_element_type=jnp.float32)
        return (intra, produced)

    intra_all, produced_all = lax.map(span_work, jnp.arange(span_count, dtype=jnp.int32))
    totals = cumulative[:, :, -1]
    totals_first = jnp.moveaxis(totals, 1, 0)

    def advance(state_now, item):
        decay_total, produced = item
        return (jnp.exp(decay_total)[..., None, None] * state_now + produced, state_now)

    zero_state = jnp.zeros((seq_count, heads_here, HEAD_DIM, STATE), jnp.float32)
    block_end, entering_local = lax.scan(advance, zero_state, (totals_first, produced_all))
    block_total = jnp.sum(totals, axis=1)
    before_span = jnp.cumsum(totals, axis=1) - totals
    growth = jnp.exp(block_total)[..., None, None]

    def relay(turn, carried_pair):
        incoming = from_behind(carried_pair[1], "seq", 1)
        return (incoming, growth * incoming + block_end)

    incoming_state, _ = lax.fori_loop(0, lax.axis_size("seq") - 1, relay, (zero_state, block_end))
    entering = (
        entering_local
        + jnp.exp(jnp.moveaxis(before_span, 1, 0))[..., None, None] * incoming_state[None]
    )
    entering_b = entering.astype(jnp.bfloat16)
    inter = jnp.einsum("scqn,cshpn->scqhp", c_spans, entering_b, preferred_element_type=jnp.float32)
    intra = jnp.moveaxis(intra_all, 0, 1)
    mixed = (
        intra
        + jnp.exp(cumulative)[..., None] * inter
        + skip_gain[:, None] * x_spans.astype(jnp.float32)
    )
    mixed = mixed.astype(jnp.bfloat16).reshape(seq_count, length, width)
    return lax.all_to_all(mixed, "head", split_axis=1, concat_axis=2, tiled=True)


def solution(mesh):
    return jax.shard_map(
        local,
        mesh=mesh,
        in_specs=(
            P(None, ("seq", "head"), None),
            P(None, ("seq", "head"), None),
            P(None, ("seq", "head"), None),
            P("head"),
            P("head"),
            P("head"),
            P(None, "head"),
            P("head"),
            P(),
            P(),
        ),
        out_specs=P(None, ("seq", "head"), None),
        check_vma=False,
    )
```

profile of v0, /device:TPU:129, one launch (start us, length us, event | category | flops | bytes accessed | tf_op | source)
XLA Modules:
  0.0 622.9 jit_solution(12799777800667414941)
XLA Ops:
  1.7 7.8 %all-to-all-start.2 = ((bf16[32,2,512]{2,1,0:T(2,128)(2,1)}), bf16[32,2,512]{2,1,0:T(2,128)(2,1)S(1)}, u32[]{:S(2)}, u32[]{:S(2)}) async-start(bf16[32,2,512]{2,1,0:T(2,128)(2,1)} %reshape.173), calls=%async_computation.2 | async-start | bytes 131072 | tf_op jit(solution)/shard_map/all_to_all | solution.py:55
  9.5 1.5 copy.123
  11.0 1.5 copy.80
  12.5 5.7 broadcast_in_dim.20
  18.1 13.9 %reshape.171 = bf16[32,2,32768]{2,1,0:T(2,128)(2,1)} reshape(bf16[16384,2,64]{2,1,0:T(2,128)(2,1)} %bitcast.187) | data formatting | bytes 8388608
  32.0 7.4 %all-to-all-start.1 = ((bf16[32,2,32768]{2,1,0:T(2,128)(2,1)}), bf16[32,2,32768]{2,1,0:T(2,128)(2,1)}, u32[]{:S(2)}, u32[]{:S(2)}) async-start(bf16[32,2,32768]{2,1,0:T(2,128)(2,1)} %reshape.171), calls=%async_computation.1 | async-start | bytes 8388608 | tf_op jit(solution)/shard_map/all_to_all | solution.py:56
  39.4 17.8 %copy.77 = bf16[2,64,16384]{1,0,2:T(2,128)(2,1)} copy(bf16[2,64,16384]{2,1,0:T(8,128)(2,1)} %param.16) | data formatting | bytes 8388608 | tf_op args[0]
  57.2 13.9 %reshape.169 = bf16[32,2,32768]{2,1,0:T(2,128)(2,1)} reshape(bf16[16384,2,64]{2,1,0:T(2,128)(2,1)} %bitcast.190) | data formatting | bytes 8388608
  71.1 20.5 %all-to-all-done.1 = bf16[32,2,32768]{2,1,0:T(2,128)(2,1)} async-done(((bf16[32,2,32768]{2,1,0:T(2,128)(2,1)}), bf16[32,2,32768]{2,1,0:T(2,128)(2,1)}, u32[]{:S(2)}, u32[]{:S(2)}) %all-to-all-start.1) | async-done | bytes 4194336 | tf_op jit(solution)/shard_map/all_to_all | solution.py:56
  91.6 7.2 %all-to-all-start = ((bf16[32,2,32768]{2,1,0:T(2,128)(2,1)}), bf16[32,2,32768]{2,1,0:T(2,128)(2,1)}, u32[]{:S(2)}, u32[]{:S(2)}) async-start(bf16[32,2,32768]{2,1,0:T(2,128)(2,1)} %reshape.169), calls=%async_computation | async-start | bytes 8388608 | tf_op jit(solution)/shard_map/all_to_all | solution.py:54
  99.6 9.0 %reduce-window.6 = f32[2,8,8,2,128]{4,2,3,1,0:T(8,128)S(1)} reduce-window(f32[2,8,8,2,128]{4,2,3,1,0:T(8,128)S(1)} %copy.86, f32[]{:T(128)} %constant.75.clone.1), window={size=1x1x1x1x128 pad=0_0x0_0x0_0x0_0x127_0}, to_apply=%region_0.1 | reduce-window | flops 4161536 | bytes 262148 | tf_op jit(solution)/shard_map/reduce-window
  109.4 13.7 %reshape.172 = bf16[16384,2,64]{2,1,0:T(2,128)(2,1)} reshape(bf16[32,2,32768]{2,1,0:T(2,128)(2,1)} %all-to-all-done.1) | data formatting | bytes 8388608
  123.1 18.5 %copy.106 = bf16[2,64,32,512]{3,1,2,0:T(8,128)(2,1)} copy(bf16[2,64,32,512]{1,0,3,2:T(2,128)(2,1)} %bitcast.188) | data formatting | bytes 8388608 | tf_op jit(solution)/shard_map/all_to_all | solution.py:56
  142.4 2.6 collective-permute-start.2
  145.0 6.0 all-to-all-done
  151.0 13.7 %reshape.170 = bf16[16384,2,64]{2,1,0:T(2,128)(2,1)} reshape(bf16[32,2,32768]{2,1,0:T(2,128)(2,1)} %all-to-all-done) | data formatting | bytes 8388608
  164.7 18.5 %copy.78 = bf16[2,64,32,512]{3,1,2,0:T(8,128)(2,1)} copy(bf16[2,64,32,512]{1,0,3,2:T(2,128)(2,1)} %bitcast.189) | data formatting | bytes 8388608 | tf_op jit(solution)/shard_map/all_to_all | solution.py:54
  183.9 2.8 collective-permute-start.1
  186.8 10.9 %multiply_convert_fusion.8 = bf16[2,2048,512]{2,1,0:T(8,128)(2,1)S(1)} fusion(bf16[2,2048,512]{2,1,0:T(8,128)(2,1)} %bitcast.192, bf16[2,3,512]{2,1,0:T(4,128)(2,1)S(1)} %collective-permute-done.2, f32[512]{0:T(512)S(1)} %bitcast.210, f32[512]{0:T(512)S(1)} %bitcast.208, f32[512]{0:T(512)S(1)} %bitcast.209, f32[512]{0:T(512)S(1)} %bitcast.207, ...), kind=kLoop, calls=%fused_computation.44 | loop fusion | flops 54525952 | bytes 8404992 | tf_op jit(solution)/shard_map/convert_element_type | solution.py:26
  197.7 2.3 fusion.41
  200.0 7.0 %multiply_convert_fusion.9 = bf16[2,2048,512]{2,1,0:T(8,128)(2,1)} fusion(bf16[2,2048,512]{2,1,0:T(8,128)(2,1)S(1)} %bitcast.194, bf16[2,3,512]{2,1,0:T(4,128)(2,1)S(1)} %collective-permute-done.1, f32[512]{0:T(512)S(1)} %bitcast.214, f32[512]{0:T(512)S(1)} %bitcast.215, f32[512]{0:T(512)S(1)} %bitcast.213, f32[512]{0:T(512)S(1)} %bitcast.212, ...), kind=kLoop, calls=%fused_computation.45 | loop fusion | flops 54525952 | bytes 8404992 | tf_op jit(solution)/shard_map/convert_element_type | solution.py:26
  207.0 6.3 %copy.79 = bf16[2,2048,512]{1,2,0:T(8,128)(2,1)} copy(bf16[2,2048,512]{2,1,0:T(8,128)(2,1)} %multiply_convert_fusion.9) | data formatting | bytes 8388608 | tf_op jit(solution)/shard_map/convert_element_type | solution.py:26
  213.3 3.7 copy.121
  217.0 3.4 copy.89
  220.4 4.3 broadcast.35.clone
  224.7 85.7 %while.39 = (s32[]{:T(128)}, f32[8,2,256,8,64]{2,4,3,0,1:T(8,128)}, f32[8,2,8,64,256]{4,3,2,1,0:T(8,128)}, s32[8]{0:T(128)S(1)}, bf16[2,8,256,8,64]{2,4,3,0,1:T(...) while((s32[]{:T(128)}, f32[8,2,256,8,64]{2,4,3,0,1:T(8,128)}, ...), condition=%wide.region_3.4_spmd.clone, body=%wide.region_2.3_spmd.clone.sunk | while | flops 342695936 | bytes 5459311 | solution.py:101
  229.1 3.5 fusion.55
  232.9 2.5 fusion.56
  239.9 3.5 fusion.55
  243.7 2.4 fusion.56
  250.5 3.6 fusion.55
  254.4 2.4 fusion.56
  261.2 3.6 fusion.55
  265.1 2.4 fusion.56
  271.9 3.6 fusion.55
  275.8 2.5 fusion.56
  282.7 3.6 fusion.55
  286.6 2.4 fusion.56
  293.4 3.5 fusion.55
  297.2 2.4 fusion.56
  304.1 3.6 fusion.55
  308.0 2.4 fusion.56
  310.4 4.3 broadcast.35
  314.6 20.5 %while.40 = (s32[]{:T(128)}, f32[2,8,64,256]{3,2,1,0:T(8,128)S(1)}, f32[8,2,8,64,256]{4,3,2,1,0:T(8,128)}, f32[8,2,8]{2,0,1:T(8,128)S(1)}, f32[8,2,8,64,256]{4,3,2,1,0:T(8,128)}, /*index=5*/s32[]{:T(128)}, s32[]{:T(128)}) while((s32[]{:T(128)}, f32[2,8,64,256]{3,2,1,0:T(8,128)S(1)}, f32[8,2,8,64,256]{4,3,2,1,0:T(8,128)}, ...), condition=%wide.region_5.6_spmd.clone, body=%wide.region_4.5_spmd.clone.sunk | while | flops 1048579 | bytes 5243808 | solution.py:110
  335.2 173.6 %while.38 = (s32[]{:T(128)}, f32[2,8,64,256]{3,2,1,0:T(8,128)}, f32[2,8,64,256]{3,2,1,0:T(8,128)S(1)}, f32[2,8,1,1]{1,0,3,2:T(2,128)S(1)}, f32[2,8,64,256]{3,2,1,0:T(8,128)S(1)}, /*index=5*/s32[]{:T(128)}) while((s32[]{:T(128)}, f32[2,8,64,256]{3,2,1,0:T(8,128)}, f32[2,8,64,256]{3,2,1,0:T(8,128)S(1)}, f32[2,8,1,1]{1,0,3,2:T(2,128)S(1)}, ...), condition=%wide.region_9.10_spmd, body=%wide.region_8.9_spmd.sunk | while | flops 524290 | bytes 11534537 | solution.py:119
  335.2 2.6 collective-permute-start
  337.9 23.9 %collective-permute-done = f32[2,8,64,256]{3,2,1,0:T(8,128)S(1)} collective-permute-done((f32[2,8,64,256]{3,2,1,0:T(8,128)S(1)}, f32[2,8,64,256]{3,2,1,0:T(8,128)S(1)}, u32[]{:S(2)}, u32[]{:S(2)}) %collective-permute-start) | collective-permute-done | bytes 1048608 | tf_op jit(solution)/shard_map/while/body/eval_jaxpr/ppermute | solution.py:16
  362.8 1.9 collective-permute-start
  364.7 23.7 %collective-permute-done = f32[2,8,64,256]{3,2,1,0:T(8,128)S(1)} collective-permute-done((f32[2,8,64,256]{3,2,1,0:T(8,128)S(1)}, f32[2,8,64,256]{3,2,1,0:T(8,128)S(1)}, u32[]{:S(2)}, u32[]{:S(2)}) %collective-permute-start) | collective-permute-done | bytes 1048608 | tf_op jit(solution)/shard_map/while/body/eval_jaxpr/ppermute | solution.py:16
  389.5 1.9 collective-permute-start
  391.4 22.8 %collective-permute-done = f32[2,8,64,256]{3,2,1,0:T(8,128)S(1)} collective-permute-done((f32[2,8,64,256]{3,2,1,0:T(8,128)S(1)}, f32[2,8,64,256]{3,2,1,0:T(8,128)S(1)}, u32[]{:S(2)}, u32[]{:S(2)}) %collective-permute-start) | collective-permute-done | bytes 1048608 | tf_op jit(solution)/shard_map/while/body/eval_jaxpr/ppermute | solution.py:16
  415.2 1.9 collective-permute-start
  417.1 21.9 %collective-permute-done = f32[2,8,64,256]{3,2,1,0:T(8,128)S(1)} collective-permute-done((f32[2,8,64,256]{3,2,1,0:T(8,128)S(1)}, f32[2,8,64,256]{3,2,1,0:T(8,128)S(1)}, u32[]{:S(2)}, u32[]{:S(2)}) %collective-permute-start) | collective-permute-done | bytes 1048608 | tf_op jit(solution)/shard_map/while/body/eval_jaxpr/ppermute | solution.py:16
  440.0 1.9 collective-permute-start
  441.9 21.0 %collective-permute-done = f32[2,8,64,256]{3,2,1,0:T(8,128)S(1)} collective-permute-done((f32[2,8,64,256]{3,2,1,0:T(8,128)S(1)}, f32[2,8,64,256]{3,2,1,0:T(8,128)S(1)}, u32[]{:S(2)}, u32[]{:S(2)}) %collective-permute-start) | collective-permute-done | bytes 1048608 | tf_op jit(solution)/shard_map/while/body/eval_jaxpr/ppermute | solution.py:16
  463.9 1.9 collective-permute-start
  465.8 20.1 %collective-permute-done = f32[2,8,64,256]{3,2,1,0:T(8,128)S(1)} collective-permute-done((f32[2,8,64,256]{3,2,1,0:T(8,128)S(1)}, f32[2,8,64,256]{3,2,1,0:T(8,128)S(1)}, u32[]{:S(2)}, u32[]{:S(2)}) %collective-permute-start) | collective-permute-done | bytes 1048608 | tf_op jit(solution)/shard_map/while/body/eval_jaxpr/ppermute | solution.py:16
  486.8 1.9 collective-permute-start
  488.7 19.1 %collective-permute-done = f32[2,8,64,256]{3,2,1,0:T(8,128)S(1)} collective-permute-done((f32[2,8,64,256]{3,2,1,0:T(8,128)S(1)}, f32[2,8,64,256]{3,2,1,0:T(8,128)S(1)}, u32[]{:S(2)}, u32[]{:S(2)}) %collective-permute-start) | collective-permute-done | bytes 1048608 | tf_op jit(solution)/shard_map/while/body/eval_jaxpr/ppermute | solution.py:16
  508.9 11.4 %fusion.29 = bf16[2,8,256,8,64]{2,4,3,1,0:T(8,128)(2,1)} fusion(f32[8,2,256,8,64]{2,4,3,0,1:T(8,128)} %get-tuple-element.112, bf16[2,8,256,8,64]{2,1,4,3,0:T(8,128)(2,1)} %bitcast.186, f32[8]{0:T(128)S(1)} %copy-done.7, f32[2,8,256,8]{2,3,1,0:T(8,128)S(1)} %get-tuple-element.251, bf16[2,8,256,256,1]{3,2,4,1,0:T(8,128)(2,1)} %bitcast.33, ...), kind=kOutput, calls=%fused_computation.42 | convolution fusion | flops 1092616192 | bytes 28443168 | tf_op jit(solution)/shard_map/scqn,cshpn->scqhp/dot_general | solution.py:125
  520.2 10.9 %copy.107 = bf16[2,8,256,8,64]{4,3,0,2,1:T(8,128)(2,1)} copy(bf16[2,8,256,8,64]{2,4,3,1,0:T(8,128)(2,1)} %fusion.29) | data formatting | bytes 8388608 | tf_op jit(solution)/shard_map/reshape | solution.py:132
  531.2 13.1 %reshape.167 = bf16[2,2048,512]{2,0,1:T(2,128)(2,1)} reshape(bf16[2,8,256,8,64]{4,3,0,2,1:T(8,128)(2,1)} %copy.107) | data formatting | bytes 8388608 | tf_op jit(solution)/shard_map/reshape | solution.py:132
  544.2 75.5 %all_to_all.63 = bf16[2,2048,512]{2,0,1:T(2,128)(2,1)S(1)} all-to-all(bf16[2,2048,512]{2,0,1:T(2,128)(2,1)} %reshape.167), channel_id=1, replica_groups=mesh['seq'=8,'head'=32] {'head'}, dimensions={1} | all-to-all | bytes 8388608 | tf_op jit(solution)/shard_map/all_to_all | solution.py:133
  620.5 2.5 copy.120
  (202 shorter events, 55.0 us)
Async XLA Ops:
  1.7 30.3 %all-to-all-start.2 = ((bf16[32,2,512]{2,1,0:T(2,128)(2,1)}), bf16[32,2,512]{2,1,0:T(2,128)(2,1)S(1)}, u32[]{:S(2)}, u32[]{:S(2)}) async-start(bf16[32,2,512]{2,1,0:T(2,128)(2,1)} %reshape.173), calls=%async_computation.2 | async-start | bytes 131072 | tf_op jit(solution)/shard_map/all_to_all | solution.py:55
  32.0 59.7 %all-to-all-start.1 = ((bf16[32,2,32768]{2,1,0:T(2,128)(2,1)}), bf16[32,2,32768]{2,1,0:T(2,128)(2,1)}, u32[]{:S(2)}, u32[]{:S(2)}) async-start(bf16[32,2,32768]{2,1,0:T(2,128)(2,1)} %reshape.171), calls=%async_computation.1 | async-start | bytes 8388608 | tf_op jit(solution)/shard_map/all_to_all | solution.py:56
  57.2 41.7 %copy-start.3 = (bf16[4,4096]{1,0:T(4,128)(2,1)S(1)}, bf16[4,4096]{1,0:T(4,128)(2,1)}, u32[]{:S(2)}) copy-start(bf16[4,4096]{1,0:T(4,128)(2,1)} %param.24) | copy-start | bytes 98308
  57.2 41.7 %copy-start.4 = (f32[4096]{0:T(1024)S(1)}, f32[4096]{0:T(1024)}, u32[]{:S(2)}) copy-start(f32[4096]{0:T(1024)} %param.25) | copy-start | bytes 49156
  57.2 41.8 %copy-start.5 = (bf16[4,512]{1,0:T(4,128)(2,1)S(1)}, bf16[4,512]{1,0:T(4,128)(2,1)}, u32[]{:S(2)}) copy-start(bf16[4,512]{1,0:T(4,128)(2,1)} %param.22) | copy-start | bytes 12292
  57.2 42.2 %copy-start.8 = (f32[8]{0:T(128)S(1)}, f32[8]{0:T(128)}, u32[]{:S(2)}) copy-start(f32[8]{0:T(128)} %param.20) | copy-start | bytes 100
  57.2 42.2 %copy-start.9 = (f32[8]{0:T(128)S(1)}, f32[8]{0:T(128)}, u32[]{:S(2)}) copy-start(f32[8]{0:T(128)} %param.19) | copy-start | bytes 100
  91.6 59.4 %all-to-all-start = ((bf16[32,2,32768]{2,1,0:T(2,128)(2,1)}), bf16[32,2,32768]{2,1,0:T(2,128)(2,1)}, u32[]{:S(2)}, u32[]{:S(2)}) async-start(bf16[32,2,32768]{2,1,0:T(2,128)(2,1)} %reshape.169), calls=%async_computation | async-start | bytes 8388608 | tf_op jit(solution)/shard_map/all_to_all | solution.py:54
  142.4 44.4 %collective-permute-start.2 = (bf16[2,3,512]{2,1,0:T(4,128)(2,1)S(1)}, bf16[2,3,512]{2,1,0:T(4,128)(2,1)S(1)}, u32[]{:S(2)}, u32[]{:S(2)}) collective-permute-start(bf16[2,3,512]{2,1,0:T(4,128)(2,1)S(1)} %slice.98), channel_id=1, source_target_pairs={{0,32},{32,64},{64,96},{96,128},{128,160},{160,192},{192,224},{1,3... | collective-permute-start | bytes 18440 | tf_op jit(solution)/shard_map/ppermute | solution.py:16
  183.9 16.1 %collective-permute-start.1 = (bf16[2,3,512]{2,1,0:T(4,128)(2,1)S(1)}, bf16[2,3,512]{2,1,0:T(4,128)(2,1)S(1)}, u32[]{:S(2)}, u32[]{:S(2)}) collective-permute-start(bf16[2,3,512]{2,1,0:T(4,128)(2,1)S(1)} %slice.93), channel_id=1, source_target_pairs={{0,32},{32,64},{64,96},{96,128},{128,160},{160,192},{192,224},{1,3... | collective-permute-start | bytes 18440 | tf_op jit(solution)/shard_map/ppermute | solution.py:16
  186.7 13.2 %copy-start.2 = (bf16[2,64,32,512]{3,1,2,0:T(8,128)(2,1)S(1)}, bf16[2,64,32,512]{3,1,2,0:T(8,128)(2,1)}, u32[]{:S(2)}) copy-start(bf16[2,64,32,512]{3,1,2,0:T(8,128)(2,1)} %copy.78) | copy-start | bytes 12582916
  186.8 13.2 %copy-start.6 = (f32[512]{0:T(512)S(1)}, f32[512]{0:T(512)}, u32[]{:S(2)}) copy-start(f32[512]{0:T(512)} %param.23) | copy-start | bytes 6148
  217.0 7.7 %copy-start = (bf16[128,8,8,256]{3,2,1,0:T(8,128)(2,1)}, bf16[128,8,8,256]{3,2,1,0:T(8,128)(2,1)S(1)}, u32[]{:S(2)}) copy-start(bf16[128,8,8,256]{3,2,1,0:T(8,128)(2,1)S(1)} %copy.121) | copy-start | bytes 12582916
  335.2 173.7 %copy-start.7 = (f32[8]{0:T(128)S(1)}, f32[8]{0:T(128)}, u32[]{:S(2)}) copy-start(f32[8]{0:T(128)} %param.21) | copy-start | bytes 100
  335.2 26.6 %collective-permute-start = (f32[2,8,64,256]{3,2,1,0:T(8,128)S(1)}, f32[2,8,64,256]{3,2,1,0:T(8,128)S(1)}, u32[]{:S(2)}, u32[]{:S(2)}) collective-permute-start(f32[2,8,64,256]{3,2,1,0:T(8,128)S(1)} %get-tuple-element.445), channel_id=1, source_target_pairs={{0,32},{32,64},{64,96},{96,128},{128,160},{160,192},{192,224},{1,3... | collective-permute-start | bytes 3145736 | tf_op jit(solution)/shard_map/while/body/eval_jaxpr/ppermute | solution.py:16
  361.8 1.0 copy-start.1
  362.8 25.7 %collective-permute-start = (f32[2,8,64,256]{3,2,1,0:T(8,128)S(1)}, f32[2,8,64,256]{3,2,1,0:T(8,128)S(1)}, u32[]{:S(2)}, u32[]{:S(2)}) collective-permute-start(f32[2,8,64,256]{3,2,1,0:T(8,128)S(1)} %get-tuple-element.445), channel_id=1, source_target_pairs={{0,32},{32,64},{64,96},{96,128},{128,160},{160,192},{192,224},{1,3... | collective-permute-start | bytes 3145736 | tf_op jit(solution)/shard_map/while/body/eval_jaxpr/ppermute | solution.py:16
  388.5 1.0 copy-start.1
  389.5 24.7 %collective-permute-start = (f32[2,8,64,256]{3,2,1,0:T(8,128)S(1)}, f32[2,8,64,256]{3,2,1,0:T(8,128)S(1)}, u32[]{:S(2)}, u32[]{:S(2)}) collective-permute-start(f32[2,8,64,256]{3,2,1,0:T(8,128)S(1)} %get-tuple-element.445), channel_id=1, source_target_pairs={{0,32},{32,64},{64,96},{96,128},{128,160},{160,192},{192,224},{1,3... | collective-permute-start | bytes 3145736 | tf_op jit(solution)/shard_map/while/body/eval_jaxpr/ppermute | solution.py:16
  414.2 1.0 copy-start.1
  415.2 23.8 %collective-permute-start = (f32[2,8,64,256]{3,2,1,0:T(8,128)S(1)}, f32[2,8,64,256]{3,2,1,0:T(8,128)S(1)}, u32[]{:S(2)}, u32[]{:S(2)}) collective-permute-start(f32[2,8,64,256]{3,2,1,0:T(8,128)S(1)} %get-tuple-element.445), channel_id=1, source_target_pairs={{0,32},{32,64},{64,96},{96,128},{128,160},{160,192},{192,224},{1,3... | collective-permute-start | bytes 3145736 | tf_op jit(solution)/shard_map/while/body/eval_jaxpr/ppermute | solution.py:16
  439.0 1.0 copy-start.1
  440.0 22.9 %collective-permute-start = (f32[2,8,64,256]{3,2,1,0:T(8,128)S(1)}, f32[2,8,64,256]{3,2,1,0:T(8,128)S(1)}, u32[]{:S(2)}, u32[]{:S(2)}) collective-permute-start(f32[2,8,64,256]{3,2,1,0:T(8,128)S(1)} %get-tuple-element.445), channel_id=1, source_target_pairs={{0,32},{32,64},{64,96},{96,128},{128,160},{160,192},{192,224},{1,3... | collective-permute-start | bytes 3145736 | tf_op jit(solution)/shard_map/while/body/eval_jaxpr/ppermute | solution.py:16
  462.9 1.0 copy-start.1
  463.9 22.0 %collective-permute-start = (f32[2,8,64,256]{3,2,1,0:T(8,128)S(1)}, f32[2,8,64,256]{3,2,1,0:T(8,128)S(1)}, u32[]{:S(2)}, u32[]{:S(2)}) collective-permute-start(f32[2,8,64,256]{3,2,1,0:T(8,128)S(1)} %get-tuple-element.445), channel_id=1, source_target_pairs={{0,32},{32,64},{64,96},{96,128},{128,160},{160,192},{192,224},{1,3... | collective-permute-start | bytes 3145736 | tf_op jit(solution)/shard_map/while/body/eval_jaxpr/ppermute | solution.py:16
  485.8 1.0 copy-start.1
  486.8 21.1 %collective-permute-start = (f32[2,8,64,256]{3,2,1,0:T(8,128)S(1)}, f32[2,8,64,256]{3,2,1,0:T(8,128)S(1)}, u32[]{:S(2)}, u32[]{:S(2)}) collective-permute-start(f32[2,8,64,256]{3,2,1,0:T(8,128)S(1)} %get-tuple-element.445), channel_id=1, source_target_pairs={{0,32},{32,64},{64,96},{96,128},{128,160},{160,192},{192,224},{1,3... | collective-permute-start | bytes 3145736 | tf_op jit(solution)/shard_map/while/body/eval_jaxpr/ppermute | solution.py:16
  507.9 1.0 copy-start.1
where the time goes:
time: 628 us; the launch traced here: 623 us
  local copies, waits for them, and re-layouts  190 us (30%)
  waiting for transfers between devices  179 us (29%)
  blocking collectives  75.5 us (12%)
  matrix products  69.6 us (11%)
  other arithmetic  50.7 us (8%)
  starting transfers between devices  41.9 us (7%)
  loops' own time  15.6 us (2%)
    ppermute x9, waiting for transfers between devices, from_behind(): return lax.ppermute(array, axis, pairs)  153 us
    unnamed x31, local copies, waits for them, and re-layouts  83.4 us
    all_to_all x1, blocking collectives, local(): lax.all_to_all(mixed, 'head', split_axis=1, concat_axis=2, tiled=True)  75.5 us
    dot_general x8, matrix products, span_work(): jnp.einsum('shtk,skhp->sthp', weights, x_here, preferred_element_type=jnp...  28.4 us
    reshape x2, local copies, waits for them, and re-layouts, local(): mixed = mixed.astype(jnp.bfloat16).reshape(seq_count, length, width)  24 us
    all_to_all x1, waiting for transfers between devices, local(): lax.all_to_all(sent_maps, 'head', split_axis=2, concat_axis=1, tiled=True)  20.5 us
    ppermute x9, starting transfers between devices, from_behind(): return lax.ppermute(array, axis, pairs)  19.5 us
    dot_general x8, matrix products, span_work(): jnp.einsum('skhp,skn->shpn', carried, b_here, preferred_element_type=jnp....  19.4 us
  transfers between devices with their start and end apart: 12, of which 9 were waited for; matrix products, arithmetic and copies ran while one was open for 23% of the time, Pallas kernels for 0%

commit v1 on v0

--- a/solution.py
+++ b/solution.py
@@ -51,7 +51,12 @@
     )
     sent_maps = spread.reshape(seq_count, row_count, head_count * 2 * STATE)
     local_x, local_step, local_maps = (
-        lax.all_to_all(projected, "head", split_axis=2, concat_axis=1, tiled=True),
+        jnp.concatenate(
+            lax.all_to_all(
+                jnp.stack(jnp.split(projected, lax.axis_size("head"), axis=2)), "head", 0, 0
+            ),
+            axis=1,
+        ),
         lax.all_to_all(step_raw, "head", split_axis=2, concat_axis=1, tiled=True),
         lax.all_to_all(sent_maps, "head", split_axis=2, concat_axis=1, tiled=True),
     )

time: 628 us -> 613 us (0.976)
  local copies, waits for them, and re-layouts: 190 us -> 177 us
    all_to_all x1, local copies, waits for them, and re-layouts: 18.5 us -> 2.82 us  [local(): lax.all_to_all(jnp.stack(jnp.split(projected, lax.axis_size('head'), axis...]
    unnamed x31 -> x61, local copies, waits for them, and re-layouts: 83.4 us -> 85.5 us
  transfers between devices with their start and end apart: 12 -> 12, of which waited for: 9 -> 9; matrix products, arithmetic and copies ran while one was open for 23% -> 21% of each run, Pallas kernels for 0% -> 0%
where the time goes in v1:
time: 613 us; the launch traced here: 609 us
  waiting for transfers between devices  183 us (30%)
  local copies, waits for them, and re-layouts  177 us (29%)
  blocking collectives  75.6 us (12%)
  matrix products  69.5 us (11%)
  other arithmetic  45.9 us (7%)
  starting transfers between devices  41.9 us (7%)
  loops' own time  15.7 us (3%)
    ppermute x9, waiting for transfers between devices, from_behind(): return lax.ppermute(array, axis, pairs)  153 us
    unnamed x61, local copies, waits for them, and re-layouts  85.5 us
    all_to_all x1, blocking collectives, local(): lax.all_to_all(mixed, 'head', split_axis=1, concat_axis=2, tiled=True)  75.6 us
    dot_general x8, matrix products, span_work(): jnp.einsum('shtk,skhp->sthp', weights, x_here, preferred_element_type=jnp...  28.4 us
    reshape x2, local copies, waits for them, and re-layouts, local(): mixed = mixed.astype(jnp.bfloat16).reshape(seq_count, length, width)  24 us
    all_to_all x1, waiting for transfers between devices, local(): lax.all_to_all(sent_maps, 'head', split_axis=2, concat_axis=1, tiled=True)  24 us
    ppermute x9, starting transfers between devices, from_behind(): return lax.ppermute(array, axis, pairs)  19.6 us
    dot_general x8, matrix products, span_work(): jnp.einsum('skhp,skn->shpn', carried, b_here, preferred_element_type=jnp....  19.4 us
  transfers between devices with their start and end apart: 12, of which 9 were waited for; matrix products, arithmetic and copies ran while one was open for 21% of the time, Pallas kernels for 0%

profile of v1, /device:TPU:129, one launch (start us, length us, event | category | flops | bytes accessed | tf_op | source)
XLA Modules:
  0.0 608.7 jit_solution(14639581643695998523)
XLA Ops:
  1.8 7.8 %all-to-all-start.2 = ((bf16[32,2,512]{2,1,0:T(2,128)(2,1)}), bf16[32,2,512]{2,1,0:T(2,128)(2,1)S(1)}, u32[]{:S(2)}, u32[]{:S(2)}) async-start(bf16[32,2,512]{2,1,0:T(2,128)(2,1)} %reshape.179), calls=%async_computation.2 | async-start | bytes 131072 | tf_op jit(solution)/shard_map/all_to_all | solution.py:60
  9.6 1.6 bitcast_dynamic-update-slice_fusion.32
  14.3 1.6 bitcast_dynamic-update-slice_fusion.29
  33.3 5.6 broadcast_in_dim.20
  38.9 13.9 %reshape.177 = bf16[32,2,32768]{2,1,0:T(2,128)(2,1)} reshape(bf16[16384,2,64]{2,1,0:T(2,128)(2,1)} %bitcast.248) | data formatting | bytes 8388608
  52.8 7.4 %all-to-all-start.1 = ((bf16[32,2,32768]{2,1,0:T(2,128)(2,1)}), bf16[32,2,32768]{2,1,0:T(2,128)(2,1)}, u32[]{:S(2)}, u32[]{:S(2)}) async-start(bf16[32,2,32768]{2,1,0:T(2,128)(2,1)} %reshape.177), calls=%async_computation.1 | async-start | bytes 8388608 | tf_op jit(solution)/shard_map/all_to_all | solution.py:61
  60.3 1.6 bitcast_dynamic-update-slice_fusion.18
  71.2 1.6 bitcast_dynamic-update-slice_fusion.11
  82.2 1.6 bitcast_dynamic-update-slice_fusion.4
  88.5 24.0 %all-to-all-done.1 = bf16[32,2,32768]{2,1,0:T(2,128)(2,1)} async-done(((bf16[32,2,32768]{2,1,0:T(2,128)(2,1)}), bf16[32,2,32768]{2,1,0:T(2,128)(2,1)}, u32[]{:S(2)}, u32[]{:S(2)}) %all-to-all-start.1) | async-done | bytes 4194336 | tf_op jit(solution)/shard_map/all_to_all | solution.py:61
  112.5 7.2 %all-to-all-start = ((bf16[32,2,64,512]{3,2,1,0:T(8,128)(2,1)}), bf16[32,2,64,512]{3,2,1,0:T(8,128)(2,1)}, u32[]{:S(2)}, u32[]{:S(2)}) async-start(bf16[32,2,64,512]{3,2,1,0:T(8,128)(2,1)} %bitcast_dynamic-update-slice_fusion.1), calls=%async_computation | async-start | bytes 8388608 | tf_op jit(solution)/shard_map/all_to_all | solution.py:55
  120.4 9.0 %reduce-window.6 = f32[2,8,8,2,128]{4,2,3,1,0:T(8,128)S(1)} reduce-window(f32[2,8,8,2,128]{4,2,3,1,0:T(8,128)S(1)} %copy.83, f32[]{:T(128)} %constant.75.clone.1), window={size=1x1x1x1x128 pad=0_0x0_0x0_0x0_0x127_0}, to_apply=%region_0.1 | reduce-window | flops 4161536 | bytes 262148 | tf_op jit(solution)/shard_map/reduce-window
  130.3 13.6 %reshape.178 = bf16[16384,2,64]{2,1,0:T(2,128)(2,1)} reshape(bf16[32,2,32768]{2,1,0:T(2,128)(2,1)} %all-to-all-done.1) | data formatting | bytes 8388608
  143.9 18.5 %copy.103 = bf16[2,64,32,512]{3,1,2,0:T(8,128)(2,1)} copy(bf16[2,64,32,512]{1,0,3,2:T(2,128)(2,1)} %bitcast.249) | data formatting | bytes 8388608 | tf_op jit(solution)/shard_map/all_to_all | solution.py:61
  163.2 2.6 collective-permute-start.2
  165.8 6.0 all-to-all-done
  171.9 2.8 copy.75
  174.7 2.8 collective-permute-start.1
  177.6 6.1 %multiply_convert_fusion.8 = bf16[2,2048,512]{2,1,0:T(8,128)(2,1)S(1)} fusion(bf16[2,2048,512]{2,1,0:T(8,128)(2,1)S(1)} %bitcast.251, bf16[2,3,512]{2,1,0:T(4,128)(2,1)S(1)} %collective-permute-done.2, f32[512]{0:T(512)S(1)} %bitcast.269, f32[512]{0:T(512)S(1)} %bitcast.267, f32[512]{0:T(512)S(1)} %bitcast.268, f32[512]{0:T(512)S(1)} %bitcast.266, ...), kind=kLoop, calls=%fused_computation.44 | loop fusion | flops 54525952 | bytes 8404992 | tf_op jit(solution)/shard_map/convert_element_type | solution.py:26
  183.7 2.3 fusion.41
  186.0 7.0 %multiply_convert_fusion.9 = bf16[2,2048,512]{2,1,0:T(8,128)(2,1)} fusion(bf16[2,2048,512]{2,1,0:T(8,128)(2,1)S(1)} %bitcast.253, bf16[2,3,512]{2,1,0:T(4,128)(2,1)S(1)} %collective-permute-done.1, f32[512]{0:T(512)S(1)} %bitcast.273, f32[512]{0:T(512)S(1)} %bitcast.274, f32[512]{0:T(512)S(1)} %bitcast.272, f32[512]{0:T(512)S(1)} %bitcast.271, ...), kind=kLoop, calls=%fused_computation.45 | loop fusion | flops 54525952 | bytes 8404992 | tf_op jit(solution)/shard_map/convert_element_type | solution.py:26
  193.1 6.3 %copy.76 = bf16[2,2048,512]{1,2,0:T(8,128)(2,1)} copy(bf16[2,2048,512]{2,1,0:T(8,128)(2,1)} %multiply_convert_fusion.9) | data formatting | bytes 8388608 | tf_op jit(solution)/shard_map/convert_element_type | solution.py:26
  199.4 3.7 copy.118
  203.0 3.4 copy.86
  206.4 4.3 broadcast.35.clone
  210.7 85.3 %while.39 = (s32[]{:T(128)}, f32[8,2,256,8,64]{2,4,3,0,1:T(8,128)}, f32[8,2,8,64,256]{4,3,2,1,0:T(8,128)}, s32[8]{0:T(128)S(1)}, bf16[2,8,256,8,64]{2,4,3,0,1:T(...) while((s32[]{:T(128)}, f32[8,2,256,8,64]{2,4,3,0,1:T(8,128)}, ...), condition=%wide.region_3.4_spmd.clone, body=%wide.region_2.3_spmd.clone.sunk | while | flops 342695936 | bytes 5459311 | solution.py:106
  215.1 3.5 fusion.55
  219.0 2.5 fusion.56
  225.9 3.5 fusion.55
  229.7 2.4 fusion.56
  236.5 3.6 fusion.55
  240.3 2.4 fusion.56
  247.1 3.5 fusion.55
  251.0 2.4 fusion.56
  257.8 3.6 fusion.55
  261.7 2.5 fusion.56
  268.5 3.5 fusion.55
  272.4 2.4 fusion.56
  279.2 3.5 fusion.55
  283.0 2.4 fusion.56
  289.8 3.6 fusion.55
  293.7 2.4 fusion.56
  296.1 4.3 broadcast.35
  300.4 20.5 %while.40 = (s32[]{:T(128)}, f32[2,8,64,256]{3,2,1,0:T(8,128)S(1)}, f32[8,2,8,64,256]{4,3,2,1,0:T(8,128)}, f32[8,2,8]{2,0,1:T(8,128)S(1)}, f32[8,2,8,64,256]{4,3,2,1,0:T(8,128)}, /*index=5*/s32[]{:T(128)}, s32[]{:T(128)}) while((s32[]{:T(128)}, f32[2,8,64,256]{3,2,1,0:T(8,128)S(1)}, f32[8,2,8,64,256]{4,3,2,1,0:T(8,128)}, ...), condition=%wide.region_5.6_spmd.clone, body=%wide.region_4.5_spmd.clone.sunk | while | flops 1048579 | bytes 5243808 | solution.py:115
  321.0 173.6 %while.38 = (s32[]{:T(128)}, f32[2,8,64,256]{3,2,1,0:T(8,128)}, f32[2,8,64,256]{3,2,1,0:T(8,128)S(1)}, f32[2,8,1,1]{1,0,3,2:T(2,128)S(1)}, f32[2,8,64,256]{3,2,1,0:T(8,128)S(1)}, /*index=5*/s32[]{:T(128)}) while((s32[]{:T(128)}, f32[2,8,64,256]{3,2,1,0:T(8,128)}, f32[2,8,64,256]{3,2,1,0:T(8,128)S(1)}, f32[2,8,1,1]{1,0,3,2:T(2,128)S(1)}, ...), condition=%wide.region_9.10_spmd, body=%wide.region_8.9_spmd.sunk | while | flops 524290 | bytes 11534537 | solution.py:124
  321.0 2.6 collective-permute-start
  323.6 23.9 %collective-permute-done = f32[2,8,64,256]{3,2,1,0:T(8,128)S(1)} collective-permute-done((f32[2,8,64,256]{3,2,1,0:T(8,128)S(1)}, f32[2,8,64,256]{3,2,1,0:T(8,128)S(1)}, u32[]{:S(2)}, u32[]{:S(2)}) %collective-permute-start) | collective-permute-done | bytes 1048608 | tf_op jit(solution)/shard_map/while/body/eval_jaxpr/ppermute | solution.py:16
  348.6 1.9 collective-permute-start
  350.5 23.7 %collective-permute-done = f32[2,8,64,256]{3,2,1,0:T(8,128)S(1)} collective-permute-done((f32[2,8,64,256]{3,2,1,0:T(8,128)S(1)}, f32[2,8,64,256]{3,2,1,0:T(8,128)S(1)}, u32[]{:S(2)}, u32[]{:S(2)}) %collective-permute-start) | collective-permute-done | bytes 1048608 | tf_op jit(solution)/shard_map/while/body/eval_jaxpr/ppermute | solution.py:16
  375.2 1.9 collective-permute-start
  377.1 22.8 %collective-permute-done = f32[2,8,64,256]{3,2,1,0:T(8,128)S(1)} collective-permute-done((f32[2,8,64,256]{3,2,1,0:T(8,128)S(1)}, f32[2,8,64,256]{3,2,1,0:T(8,128)S(1)}, u32[]{:S(2)}, u32[]{:S(2)}) %collective-permute-start) | collective-permute-done | bytes 1048608 | tf_op jit(solution)/shard_map/while/body/eval_jaxpr/ppermute | solution.py:16
  400.9 1.9 collective-permute-start
  402.8 21.9 %collective-permute-done = f32[2,8,64,256]{3,2,1,0:T(8,128)S(1)} collective-permute-done((f32[2,8,64,256]{3,2,1,0:T(8,128)S(1)}, f32[2,8,64,256]{3,2,1,0:T(8,128)S(1)}, u32[]{:S(2)}, u32[]{:S(2)}) %collective-permute-start) | collective-permute-done | bytes 1048608 | tf_op jit(solution)/shard_map/while/body/eval_jaxpr/ppermute | solution.py:16
  425.7 1.9 collective-permute-start
  427.6 21.0 %collective-permute-done = f32[2,8,64,256]{3,2,1,0:T(8,128)S(1)} collective-permute-done((f32[2,8,64,256]{3,2,1,0:T(8,128)S(1)}, f32[2,8,64,256]{3,2,1,0:T(8,128)S(1)}, u32[]{:S(2)}, u32[]{:S(2)}) %collective-permute-start) | collective-permute-done | bytes 1048608 | tf_op jit(solution)/shard_map/while/body/eval_jaxpr/ppermute | solution.py:16
  449.6 1.9 collective-permute-start
  451.5 20.1 %collective-permute-done = f32[2,8,64,256]{3,2,1,0:T(8,128)S(1)} collective-permute-done((f32[2,8,64,256]{3,2,1,0:T(8,128)S(1)}, f32[2,8,64,256]{3,2,1,0:T(8,128)S(1)}, u32[]{:S(2)}, u32[]{:S(2)}) %collective-permute-start) | collective-permute-done | bytes 1048608 | tf_op jit(solution)/shard_map/while/body/eval_jaxpr/ppermute | solution.py:16
  472.6 1.9 collective-permute-start
  474.5 19.1 %collective-permute-done = f32[2,8,64,256]{3,2,1,0:T(8,128)S(1)} collective-permute-done((f32[2,8,64,256]{3,2,1,0:T(8,128)S(1)}, f32[2,8,64,256]{3,2,1,0:T(8,128)S(1)}, u32[]{:S(2)}, u32[]{:S(2)}) %collective-permute-start) | collective-permute-done | bytes 1048608 | tf_op jit(solution)/shard_map/while/body/eval_jaxpr/ppermute | solution.py:16
  494.6 11.4 %fusion.29 = bf16[2,8,256,8,64]{2,4,3,1,0:T(8,128)(2,1)} fusion(f32[8,2,256,8,64]{2,4,3,0,1:T(8,128)} %get-tuple-element.112, bf16[2,8,256,8,64]{2,1,4,3,0:T(8,128)(2,1)} %bitcast.247, f32[8]{0:T(128)S(1)} %copy-done.8, f32[2,8,256,8]{2,3,1,0:T(8,128)S(1)} %get-tuple-element.251, bf16[2,8,256,256,1]{3,2,4,1,0:T(8,128)(2,1)} %bitcast.64, ...), kind=kOutput, calls=%fused_computation.42 | convolution fusion | flops 1092616192 | bytes 28443168 | tf_op jit(solution)/shard_map/scqn,cshpn->scqhp/dot_general | solution.py:130
  506.0 10.9 %copy.104 = bf16[2,8,256,8,64]{4,3,0,2,1:T(8,128)(2,1)} copy(bf16[2,8,256,8,64]{2,4,3,1,0:T(8,128)(2,1)} %fusion.29) | data formatting | bytes 8388608 | tf_op jit(solution)/shard_map/reshape | solution.py:137
  516.9 13.1 %reshape.175 = bf16[2,2048,512]{2,0,1:T(2,128)(2,1)} reshape(bf16[2,8,256,8,64]{4,3,0,2,1:T(8,128)(2,1)} %copy.104) | data formatting | bytes 8388608 | tf_op jit(solution)/shard_map/reshape | solution.py:137
  530.0 75.6 %all_to_all.50 = bf16[2,2048,512]{2,0,1:T(2,128)(2,1)S(1)} all-to-all(bf16[2,2048,512]{2,0,1:T(2,128)(2,1)} %reshape.175), channel_id=1, replica_groups=mesh['seq'=8,'head'=32] {'head'}, dimensions={1} | all-to-all | bytes 8388608 | tf_op jit(solution)/shard_map/all_to_all | solution.py:138
  606.2 2.5 copy.117
  (233 shorter events, 98.1 us)
Async XLA Ops:
  0.0 31.5 %copy-start.3 = (bf16[2,64,4096]{2,1,0:T(8,128)(2,1)S(1)}, bf16[2,64,4096]{2,1,0:T(8,128)(2,1)}, u32[]{:S(2)}) copy-start(bf16[2,64,4096]{2,1,0:T(8,128)(2,1)} %param.17) | copy-start | bytes 3145732
  1.8 51.0 %all-to-all-start.2 = ((bf16[32,2,512]{2,1,0:T(2,128)(2,1)}), bf16[32,2,512]{2,1,0:T(2,128)(2,1)S(1)}, u32[]{:S(2)}, u32[]{:S(2)}) async-start(bf16[32,2,512]{2,1,0:T(2,128)(2,1)} %reshape.179), calls=%async_computation.2 | async-start | bytes 131072 | tf_op jit(solution)/shard_map/all_to_all | solution.py:60
  52.8 59.7 %all-to-all-start.1 = ((bf16[32,2,32768]{2,1,0:T(2,128)(2,1)}), bf16[32,2,32768]{2,1,0:T(2,128)(2,1)}, u32[]{:S(2)}, u32[]{:S(2)}) async-start(bf16[32,2,32768]{2,1,0:T(2,128)(2,1)} %reshape.177), calls=%async_computation.1 | async-start | bytes 8388608 | tf_op jit(solution)/shard_map/all_to_all | solution.py:61
  88.5 31.2 %copy-start.4 = (bf16[4,4096]{1,0:T(4,128)(2,1)S(1)}, bf16[4,4096]{1,0:T(4,128)(2,1)}, u32[]{:S(2)}) copy-start(bf16[4,4096]{1,0:T(4,128)(2,1)} %param.24) | copy-start | bytes 98308
  88.5 31.3 %copy-start.5 = (f32[4096]{0:T(1024)S(1)}, f32[4096]{0:T(1024)}, u32[]{:S(2)}) copy-start(f32[4096]{0:T(1024)} %param.25) | copy-start | bytes 49156
  88.5 31.3 %copy-start.6 = (bf16[4,512]{1,0:T(4,128)(2,1)S(1)}, bf16[4,512]{1,0:T(4,128)(2,1)}, u32[]{:S(2)}) copy-start(bf16[4,512]{1,0:T(4,128)(2,1)} %param.22) | copy-start | bytes 12292
  88.5 31.7 %copy-start.9 = (f32[8]{0:T(128)S(1)}, f32[8]{0:T(128)}, u32[]{:S(2)}) copy-start(f32[8]{0:T(128)} %param.20) | copy-start | bytes 100
  88.5 31.7 %copy-start.10 = (f32[8]{0:T(128)S(1)}, f32[8]{0:T(128)}, u32[]{:S(2)}) copy-start(f32[8]{0:T(128)} %param.19) | copy-start | bytes 100
  112.5 59.4 %all-to-all-start = ((bf16[32,2,64,512]{3,2,1,0:T(8,128)(2,1)}), bf16[32,2,64,512]{3,2,1,0:T(8,128)(2,1)}, u32[]{:S(2)}, u32[]{:S(2)}) async-start(bf16[32,2,64,512]{3,2,1,0:T(8,128)(2,1)} %bitcast_dynamic-update-slice_fusion.1), calls=%async_computation | async-start | bytes 8388608 | tf_op jit(solution)/shard_map/all_to_all | solution.py:55
  163.2 14.4 %collective-permute-start.2 = (bf16[2,3,512]{2,1,0:T(4,128)(2,1)S(1)}, bf16[2,3,512]{2,1,0:T(4,128)(2,1)S(1)}, u32[]{:S(2)}, u32[]{:S(2)}) collective-permute-start(bf16[2,3,512]{2,1,0:T(4,128)(2,1)S(1)} %slice.98), channel_id=1, source_target_pairs={{0,32},{32,64},{64,96},{96,128},{128,160},{160,192},{192,224},{1,3... | collective-permute-start | bytes 18440 | tf_op jit(solution)/shard_map/ppermute | solution.py:16
  171.9 5.7 copy-start.2
  174.7 11.3 %collective-permute-start.1 = (bf16[2,3,512]{2,1,0:T(4,128)(2,1)S(1)}, bf16[2,3,512]{2,1,0:T(4,128)(2,1)S(1)}, u32[]{:S(2)}, u32[]{:S(2)}) collective-permute-start(bf16[2,3,512]{2,1,0:T(4,128)(2,1)S(1)} %slice.93), channel_id=1, source_target_pairs={{0,32},{32,64},{64,96},{96,128},{128,160},{160,192},{192,224},{1,3... | collective-permute-start | bytes 18440 | tf_op jit(solution)/shard_map/ppermute | solution.py:16
  183.7 2.3 copy-start.7
  203.0 3.4 copy-start
  320.9 173.6 %copy-start.8 = (f32[8]{0:T(128)S(1)}, f32[8]{0:T(128)}, u32[]{:S(2)}) copy-start(f32[8]{0:T(128)} %param.21) | copy-start | bytes 100
  321.0 26.6 %collective-permute-start = (f32[2,8,64,256]{3,2,1,0:T(8,128)S(1)}, f32[2,8,64,256]{3,2,1,0:T(8,128)S(1)}, u32[]{:S(2)}, u32[]{:S(2)}) collective-permute-start(f32[2,8,64,256]{3,2,1,0:T(8,128)S(1)} %get-tuple-element.445), channel_id=1, source_target_pairs={{0,32},{32,64},{64,96},{96,128},{128,160},{160,192},{192,224},{1,3... | collective-permute-start | bytes 3145736 | tf_op jit(solution)/shard_map/while/body/eval_jaxpr/ppermute | solution.py:16
  347.6 1.0 copy-start.1
  348.6 25.7 %collective-permute-start = (f32[2,8,64,256]{3,2,1,0:T(8,128)S(1)}, f32[2,8,64,256]{3,2,1,0:T(8,128)S(1)}, u32[]{:S(2)}, u32[]{:S(2)}) collective-permute-start(f32[2,8,64,256]{3,2,1,0:T(8,128)S(1)} %get-tuple-element.445), channel_id=1, source_target_pairs={{0,32},{32,64},{64,96},{96,128},{128,160},{160,192},{192,224},{1,3... | collective-permute-start | bytes 3145736 | tf_op jit(solution)/shard_map/while/body/eval_jaxpr/ppermute | solution.py:16
  374.2 1.0 copy-start.1
  375.2 24.7 %collective-permute-start = (f32[2,8,64,256]{3,2,1,0:T(8,128)S(1)}, f32[2,8,64,256]{3,2,1,0:T(8,128)S(1)}, u32[]{:S(2)}, u32[]{:S(2)}) collective-permute-start(f32[2,8,64,256]{3,2,1,0:T(8,128)S(1)} %get-tuple-element.445), channel_id=1, source_target_pairs={{0,32},{32,64},{64,96},{96,128},{128,160},{160,192},{192,224},{1,3... | collective-permute-start | bytes 3145736 | tf_op jit(solution)/shard_map/while/body/eval_jaxpr/ppermute | solution.py:16
  399.9 1.0 copy-start.1
  400.9 23.8 %collective-permute-start = (f32[2,8,64,256]{3,2,1,0:T(8,128)S(1)}, f32[2,8,64,256]{3,2,1,0:T(8,128)S(1)}, u32[]{:S(2)}, u32[]{:S(2)}) collective-permute-start(f32[2,8,64,256]{3,2,1,0:T(8,128)S(1)} %get-tuple-element.445), channel_id=1, source_target_pairs={{0,32},{32,64},{64,96},{96,128},{128,160},{160,192},{192,224},{1,3... | collective-permute-start | bytes 3145736 | tf_op jit(solution)/shard_map/while/body/eval_jaxpr/ppermute | solution.py:16
  424.7 1.0 copy-start.1
  425.7 22.9 %collective-permute-start = (f32[2,8,64,256]{3,2,1,0:T(8,128)S(1)}, f32[2,8,64,256]{3,2,1,0:T(8,128)S(1)}, u32[]{:S(2)}, u32[]{:S(2)}) collective-permute-start(f32[2,8,64,256]{3,2,1,0:T(8,128)S(1)} %get-tuple-element.445), channel_id=1, source_target_pairs={{0,32},{32,64},{64,96},{96,128},{128,160},{160,192},{192,224},{1,3... | collective-permute-start | bytes 3145736 | tf_op jit(solution)/shard_map/while/body/eval_jaxpr/ppermute | solution.py:16
  448.6 1.0 copy-start.1
  449.6 22.0 %collective-permute-start = (f32[2,8,64,256]{3,2,1,0:T(8,128)S(1)}, f32[2,8,64,256]{3,2,1,0:T(8,128)S(1)}, u32[]{:S(2)}, u32[]{:S(2)}) collective-permute-start(f32[2,8,64,256]{3,2,1,0:T(8,128)S(1)} %get-tuple-element.445), channel_id=1, source_target_pairs={{0,32},{32,64},{64,96},{96,128},{128,160},{160,192},{192,224},{1,3... | collective-permute-start | bytes 3145736 | tf_op jit(solution)/shard_map/while/body/eval_jaxpr/ppermute | solution.py:16
  471.6 1.0 copy-start.1
  472.6 21.1 %collective-permute-start = (f32[2,8,64,256]{3,2,1,0:T(8,128)S(1)}, f32[2,8,64,256]{3,2,1,0:T(8,128)S(1)}, u32[]{:S(2)}, u32[]{:S(2)}) collective-permute-start(f32[2,8,64,256]{3,2,1,0:T(8,128)S(1)} %get-tuple-element.445), channel_id=1, source_target_pairs={{0,32},{32,64},{64,96},{96,128},{128,160},{160,192},{192,224},{1,3... | collective-permute-start | bytes 3145736 | tf_op jit(solution)/shard_map/while/body/eval_jaxpr/ppermute | solution.py:16
  493.6 1.0 copy-start.1
